TPU v7x, 32 devices: a whole 2x2x4 slice. The times are simulated.
32 devices in a mesh: tgt: 4 (over x, core), src: 8 (over z, y).
Axes of the slice: x: 2, y: 2, z: 4, core: 2. Of those that a mesh axis runs over, the one named last changes fastest.
Arguments:
- multipoles: float32 [512, 16, 128], P(('src', 'tgt')), may hold values from -6 to 6
- couplings: float32 [64, 288, 128, 128], P('tgt', 'src'), may hold values from -0.0390625 to 0.0390625
- slot_sources: int32 [64, 288], P('tgt', 'src'), may hold values from -1 to 511, as said below
Outputs:
- local_coeffs: float32 [1024, 128], P(('tgt', 'src'))
Inputs may be any that keep to these rules, and one draw needn't show every extreme that they name: `slot_sources`: columns j * 36 to (j + 1) * 36 - 1 of a row name only clusters of source block j, ids j * 16 * 4 to (j + 1) * 16 * 4 - 1, or -1. Each row names exactly 189 distinct clusters; in every row one block's 36 slots are all used.
All inputs are finite; a program needn't handle non-finite values.
Results may differ from a plain program's by a relative error of at most 0.0003.
Values sent between devices are 32-bit elements; how exact they have to be, the bound alone decides.
A program may use at most 128 MiB of HBM per device.

v0:
```python
import jax
import jax.numpy as jnp
from jax import lax
from jax.sharding import PartitionSpec as P


def body(multipoles, couplings, slot_sources):
    source_block = lax.all_gather(multipoles, "tgt", axis=0, tiled=True)
    block_size = source_block.shape[0]
    block_start = lax.axis_index("src") * block_size
    live = slot_sources >= 0
    row_index = jnp.where(live, slot_sources - block_start, 0)
    chosen = source_block[row_index]
    chosen = jnp.where(live[:, :, None, None], chosen, jnp.zeros_like(chosen))
    target_count = chosen.shape[0]
    nrhs_count = chosen.shape[2]
    rank_width = chosen.shape[3]
    partial_value = jnp.einsum("tsnr,tsrq->tnq", chosen, couplings, precision=lax.Precision.HIGHEST)
    partial_value = partial_value.reshape(target_count * nrhs_count, rank_width)
    local_coeffs = lax.psum_scatter(partial_value, "src", scatter_dimension=0, tiled=True)
    return local_coeffs


def solution(mesh):
    placed = (P(("src", "tgt"), None, None), P("tgt", "src", None, None), P("tgt", "src"))
    return jax.shard_map(
        body, mesh=mesh, in_specs=placed, out_specs=P(("tgt", "src"), None), check_vma=False
    )
```

profile of v0, /device:TPU:0, one launch (start us, length us, event | category | flops | bytes accessed | tf_op | source)
XLA Modules:
  0.0 113.8 jit_solution(5441605728410760219)
XLA Ops:
  6.5 0.0 reduce-scatter.2.cloned.1.call-start
  6.5 8.8 %all_gather.3 = f32[64,16,128]{2,1,0:T(8,128)S(1)} all-gather(f32[16,16,128]{2,1,0:T(8,128)} %param.3), channel_id=1, replica_groups=mesh['tgt'=4,'src'=8] {'tgt'}, dimensions={0}, use_global_device_ids=true | all-gather | bytes 655360 | tf_op jit(solution)/shard_map/all_gather | solution.py:8
  15.4 0.7 broadcast_compare_fusion
  16.1 0.7 compare_select_fusion
  16.8 0.1 reshape.7
  16.9 3.4 %gather_fusion = f32[576,16,128]{2,1,0:T(8,128)} fusion(f32[64,16,128]{2,1,0:T(8,128)S(1)} %all_gather.3, s32[1024]{0:T(1024)S(1)} %pad_clamp_fusion), kind=kCustom, calls=%fused_computation | custom fusion | bytes 9439488 | tf_op jit(solution)/shard_map/gather | solution.py:13
  20.3 24.1 %fusion = f32[16,16,128,1]{2,1,3,0:T(8,128)} fusion(f32[16,36,128,128]{3,2,1,0:T(8,128)} %param.4, f32[16,36,16,128]{3,2,1,0:T(8,128)} %bitcast.6, pred[16,36]{1,0:T(8,128)(4,1)S(1)} %broadcast_compare_fusion), kind=kOutput, calls=%fused_computation.1 | convolution fusion | flops 1813118976 | bytes 42598976 | tf_op jit(solution)/shard_map/tsnr,tsrq->tnq/dot_general | solution.py:18
  44.4 0.0 reduce-scatter.2.cloned.1.call-update
  44.4 62.5 %reduce-scatter.2.cloned.1.call-done = f32[32,128]{1,0:T(8,128)} async-done(((f32[256,128]{1,0:T(8,128)}), f32[32,128]{1,0:T(8,128)}) %reduce-scatter.2.cloned.1.call-update) | async-done | bytes 16400 | tf_op jit(solution)/shard_map/reduce_scatter | solution.py:20
  (1 shorter events, 0.0 us)
Async XLA Ops:
  6.5 100.4 %reduce-scatter.2.cloned.1.call-start = ((), (), s32[]{:S(2)}) async-start(), calls=%async_computation.1 | async-start | bytes 147456 | tf_op jit(solution)/shard_map/reduce_scatter | solution.py:20
Sparse Core Ops, SparseCore 0:
  44.5 62.3 reduce-scatter.1
where the time goes:
time: 114 us
  waiting for transfers between devices  62.5 us (55%)
  matrix products  24.1 us (21%)
  between operations  13.4 us (12%)
  blocking collectives  8.82 us (8%)
  local copies, waits for them, and re-layouts  3.53 us (3%)
  other arithmetic  1.41 us (1%)
    reduce_scatter x1, waiting for transfers between devices, body(): lax.psum_scatter(partial_value, 'src', scatter_dimension=0, tiled=True)  62.5 us
    dot_general x1, matrix products, body(): jnp.einsum('tsnr,tsrq->tnq', chosen, couplings, precision=lax.Precision.H...  24.1 us
    all_gather x1, blocking collectives, body(): source_block = lax.all_gather(multipoles, 'tgt', axis=0, tiled=True)  8.82 us
    gather x1, local copies, waits for them, and re-layouts, body(): chosen = source_block[row_index]  3.45 us
  transfers between devices with their start and end apart: 1, of which 1 were waited for; matrix products, arithmetic and copies ran while one was open for 0% of the time, Pallas kernels for 0%

commit v1 on v0

v1 whole, which is shorter than its diff:
```python
import functools

import jax
import jax.numpy as jnp
from jax import lax
from jax.experimental import pallas as pl
from jax.experimental.pallas import tpu as pltpu
from jax.sharding import PartitionSpec as P

MESH = pl.DeviceIdType.MESH
DEPTH = 4


def split(value):
    high = value.astype(jnp.bfloat16)
    low = (value - high.astype(jnp.float32)).astype(jnp.bfloat16)
    return high, low


def kernel(n_tgt, n_src, mult_ref, coup_ref, slot_ref, out_ref, held, gathered, panels, partial, received,
           held_sem, own_sem, gather_send, gather_recv, pass_send, pass_recv, part_send, part_recv):
    targets, slots, rank = held.shape[:3]
    clusters, nrhs = mult_ref.shape[:2]
    block = n_tgt * clusters
    rows = out_ref.shape[0]
    steps = min(n_src, targets)
    per_step = targets // steps
    owners = n_src // steps
    chips = n_tgt // 2
    my_tgt, my_src = lax.axis_index("tgt"), lax.axis_index("src")
    my_chip, my_core = my_tgt // 2, lax.rem(my_tgt, 2)
    sibling = my_chip * 2 + 1 - my_core
    my_group, my_place = my_src // owners, lax.rem(my_src, owners)

    def target_at(k):
        return lax.rem(my_group + 1 + k // per_step, steps) * per_step + lax.rem(k, per_step)

    def coupling_copy(k):
        return pltpu.make_async_copy(coup_ref.at[target_at(k)], held.at[k], held_sem.at[k])

    def same_core(hop):
        return lax.rem(my_chip + hop, chips) * 2 + my_core

    barrier = pltpu.get_barrier_semaphore()
    pl.semaphore_signal(barrier, inc=1, device_id={"tgt": sibling}, device_id_type=MESH)
    for hop in range(1, chips):
        pl.semaphore_signal(barrier, inc=1, device_id={"tgt": same_core(hop)}, device_id_type=MESH)
    for hop in range(1, n_src):
        pl.semaphore_signal(barrier, inc=1, device_id={"src": lax.rem(my_src + hop, n_src)}, device_id_type=MESH)

    own = pl.ds(my_tgt * clusters, clusters)
    own_copy = pltpu.make_async_copy(mult_ref, gathered.at[own], own_sem)
    own_copy.start()
    for k in range(min(DEPTH, targets)):
        coupling_copy(k).start()
    pl.semaphore_wait(barrier, chips + n_src - 1)

    across = []
    for hop in range(1, chips):
        copy = pltpu.make_async_remote_copy(
            src_ref=mult_ref, dst_ref=gathered.at[own], send_sem=gather_send.at[hop], recv_sem=gather_recv.at[hop],
            device_id={"tgt": same_core(hop)}, device_id_type=MESH)
        copy.start()
        across.append(copy)
    passed = [pltpu.make_async_remote_copy(
        src_ref=mult_ref, dst_ref=gathered.at[own], send_sem=pass_send.at[0], recv_sem=pass_recv.at[0],
        device_id={"tgt": sibling}, device_id_type=MESH)]
    passed[0].start()

    def fill(tgt):
        high, low = split(gathered[pl.ds(tgt * clusters, clusters)])
        at = pl.ds(tgt * clusters + 1, clusters)
        panels[at, :nrhs] = high
        panels[at, nrhs:] = low

    panels[0] = jnp.zeros((2 * nrhs, rank), jnp.bfloat16)
    own_copy.wait()
    fill(my_tgt)
    passed[0].wait_recv()
    fill(sibling)
    for hop in range(1, chips):
        across[hop - 1].wait_recv()
        origin = lax.rem(my_chip + chips - hop, chips) * 2 + my_core
        at = gathered.at[pl.ds(origin * clusters, clusters)]
        copy = pltpu.make_async_remote_copy(
            src_ref=at, dst_ref=at, send_sem=pass_send.at[hop], recv_sem=pass_recv.at[hop],
            device_id={"tgt": sibling}, device_id_type=MESH)
        copy.start()
        passed.append(copy)
        fill(origin)
    for hop in range(1, chips):
        passed[hop].wait_recv()
        fill(lax.rem(my_chip + chips - hop, chips) * 2 + 1 - my_core)

    before = my_src * block - 1

    def part_copy(dest):
        return pltpu.make_async_remote_copy(
            src_ref=partial.at[pl.ds(pl.multiple_of(dest * rows, 8), rows)], dst_ref=received.at[my_src],
            send_sem=part_send.at[dest], recv_sem=part_recv.at[my_src],
            device_id={"src": dest}, device_id_type=MESH)

    def one_target(k, carry):
        @pl.when(k + DEPTH < targets)
        def _():
            coupling_copy(k + DEPTH).start()

        target = target_at(k)
        coupling_copy(k).wait()
        total = jnp.zeros((2 * nrhs, 2 * rank), jnp.float32)
        for first in range(0, slots, 2):
            pair = range(first, min(first + 2, slots))
            chosen = []
            for s in pair:
                chosen.append(panels[jnp.maximum(slot_ref[target, s] - before, 0)])
            left = jnp.concatenate(chosen, axis=1)
            high, low = split(held[k, first:first + len(pair)].reshape(len(pair) * rank, rank))
            right = jnp.concatenate([high, low], axis=1)
            total = total + jnp.dot(left, right, preferred_element_type=jnp.float32)
        total = total[:nrhs] + total[nrhs:]
        partial[pl.ds(pl.multiple_of(target * nrhs, 8), nrhs)] = total[:, :rank] + total[:, rank:]

        step = k // per_step
        group = lax.rem(my_group + 1 + step, steps)

        @pl.when(jnp.logical_and(lax.rem(k, per_step) == per_step - 1, step < steps - 1))
        def _():
            for o in range(owners):
                part_copy(group * owners + o).start()

        return carry

    lax.fori_loop(0, targets, one_target, 0)
    for o in range(1, owners):
        part_copy(my_group * owners + lax.rem(my_place + o, owners)).start()

    result = partial[pl.ds(pl.multiple_of(my_src * rows, 8), rows)]
    for hop in range(1, n_src):
        origin = lax.rem(my_src + hop, n_src)
        pltpu.make_async_remote_copy(
            src_ref=received.at[origin], dst_ref=received.at[origin], send_sem=part_send.at[origin],
            recv_sem=part_recv.at[origin], device_id={"src": origin}, device_id_type=MESH).wait_recv()
        result = result + received[origin]
    out_ref[...] = result

    for copy in across + passed:
        copy.wait_send()
    for hop in range(1, n_src):
        part_copy(lax.rem(my_src + hop, n_src)).wait_send()


def body(n_tgt, n_src, multipoles, couplings, slot_sources):
    clusters, nrhs, rank = multipoles.shape
    targets, slots = couplings.shape[:2]
    rows = targets * nrhs // n_src
    chips = n_tgt // 2
    dma = pltpu.SemaphoreType.DMA
    return pl.pallas_call(
        functools.partial(kernel, n_tgt, n_src),
        out_shape=jax.ShapeDtypeStruct((rows, rank), jnp.float32),
        in_specs=[
            pl.BlockSpec(memory_space=pl.ANY),
            pl.BlockSpec(memory_space=pl.ANY),
            pl.BlockSpec(memory_space=pltpu.SMEM),
        ],
        out_specs=pl.BlockSpec(memory_space=pltpu.VMEM),
        scratch_shapes=[
            pltpu.VMEM((targets, slots, rank, rank), jnp.float32),
            pltpu.VMEM((n_tgt * clusters, nrhs, rank), jnp.float32),
            pltpu.VMEM((n_tgt * clusters + 1, 2 * nrhs, rank), jnp.bfloat16),
            pltpu.VMEM((targets * nrhs, rank), jnp.float32),
            pltpu.VMEM((n_src, rows, rank), jnp.float32),
            dma((targets,)),
            dma,
            dma((chips,)),
            dma((chips,)),
            dma((chips,)),
            dma((chips,)),
            dma((n_src,)),
            dma((n_src,)),
        ],
        compiler_params=pltpu.CompilerParams(
            collective_id=0, has_side_effects=True, vmem_limit_bytes=48 * 1024 * 1024),
        cost_estimate=pl.CostEstimate(
            flops=2 * targets * slots * nrhs * rank * rank, bytes_accessed=4 * targets * slots * rank * rank,
            transcendentals=0),
    )(multipoles, couplings, slot_sources)


def solution(mesh):
    placed = (P(("src", "tgt"), None, None), P("tgt", "src", None, None), P("tgt", "src"))
    return jax.shard_map(
        functools.partial(body, mesh.shape["tgt"], mesh.shape["src"]), mesh=mesh, in_specs=placed,
        out_specs=P(("tgt", "src"), None), check_vma=False
    )
```

time: 114 us -> 25.1 us (0.22)
  waiting for transfers between devices: 62.5 us -> 0 us
  matrix products: 24.1 us -> 0 us
  Pallas kernels: 0 us -> 22.7 us
  between operations: 13.4 us -> 0.01 us
  blocking collectives: 8.82 us -> 0 us
  other arithmetic: 1.41 us -> 0 us
  local copies, waits for them, and re-layouts: 3.53 us -> 2.21 us
    reduce_scatter x1 -> x0, waiting for transfers between devices: 62.5 us -> none  [body(): lax.psum_scatter(partial_value, 'src', scatter_dimension=0, tiled=True)]
    dot_general x1 -> x0, matrix products: 24.1 us -> none  [body(): jnp.einsum('tsnr,tsrq->tnq', chosen, couplings, precision=lax.Precision.H...]
    pallas_call x0 -> x1, Pallas kernels: none -> 22.7 us  [body(): pl.pallas_call(functools.partial(kernel, n_tgt, n_src), out_shape=jax.Sha...]
    all_gather x1 -> x0, blocking collectives: 8.82 us -> none  [body(): source_block = lax.all_gather(multipoles, 'tgt', axis=0, tiled=True)]
    gather x1 -> x0, local copies, waits for them, and re-layouts: 3.45 us -> none  [body(): chosen = source_block[row_index]]
    unnamed x0 -> x5, local copies, waits for them, and re-layouts: none -> 2.21 us
  transfers between devices with their start and end apart: 1 -> 0, of which waited for: 1 -> 0; matrix products, arithmetic and copies ran while one was open for 0% -> 0% of each run, Pallas kernels for 0% -> 0%
where the time goes in v1:
time: 25.1 us; the launch traced here: 24.9 us
  Pallas kernels  22.7 us (90%)
  local copies, waits for them, and re-layouts  2.21 us (9%)
    pallas_call x1, Pallas kernels, body(): pl.pallas_call(functools.partial(kernel, n_tgt, n_src), out_shape=jax.Sha...  22.7 us
    unnamed x5, local copies, waits for them, and re-layouts  2.21 us

profile of v1, /device:TPU:0, one launch (start us, length us, event | category | flops | bytes accessed | tf_op | source)
XLA Modules:
  0.0 24.9 jit_solution(16871429305583465001)
XLA Ops:
  0.0 0.0 copy-start
  0.0 0.9 %copy-done = f32[16,16,128]{2,1,0:T(8,128)S(1)} copy-done((f32[16,16,128]{2,1,0:T(8,128)S(1)}, f32[16,16,128]{2,1,0:T(8,128)}, u32[]{:S(2)}) %copy-start) | copy-done | bytes 131096
  0.9 0.0 copy-start.1
  0.9 0.7 %copy-done.1 = s32[16,36]{1,0:T(8,128)S(1)} copy-done((s32[16,36]{1,0:T(8,128)S(1)}, s32[16,36]{1,0:T(8,128)}, u32[]{:S(2)}) %copy-start.1) | copy-done | bytes 2328
  1.6 22.7 %shard_map.37 = f32[32,128]{1,0:T(8,128)S(1)} custom-call(f32[16,16,128]{2,1,0:T(8,128)S(1)} %copy-done, f32[16,36,128,128]{3,2,1,0:T(8,128)} %coup_ref.1, s32[16,36]{1,0:T(8,128)S(1)} %copy-done.1), custom_call_target="tpu_custom_call" | custom-call | flops 301989888 | bytes 37748736 | tf_op jit(solution)/shard_map/pallas_call | solution.py:158
  24.3 0.6 %copy.5 = f32[32,128]{1,0:T(8,128)} copy(f32[32,128]{1,0:T(8,128)S(1)} %shard_map.37) | data formatting | bytes 32768
Async XLA Ops:
  0.0 0.9 %copy-start = (f32[16,16,128]{2,1,0:T(8,128)S(1)}, f32[16,16,128]{2,1,0:T(8,128)}, u32[]{:S(2)}) copy-start(f32[16,16,128]{2,1,0:T(8,128)} %mult_ref.1) | copy-start | bytes 393220
  0.9 0.7 %copy-start.1 = (s32[16,36]{1,0:T(8,128)S(1)}, s32[16,36]{1,0:T(8,128)}, u32[]{:S(2)}) copy-start(s32[16,36]{1,0:T(8,128)} %slot_ref.1) | copy-start | bytes 6916

commit v2 on v1

--- a/solution.py
+++ b/solution.py
@@ -8,7 +8,9 @@
 from jax.sharding import PartitionSpec as P
 
 MESH = pl.DeviceIdType.MESH
-DEPTH = 4
+DEPTH = 8
+UNROLL = 2
+PARTS = 1
 
 
 def split(value):
@@ -17,8 +19,8 @@
     return high, low
 
 
-def kernel(n_tgt, n_src, mult_ref, coup_ref, slot_ref, out_ref, held, gathered, panels, partial, received,
-           held_sem, own_sem, gather_send, gather_recv, pass_send, pass_recv, part_send, part_recv):
+def kernel(n_tgt, n_src, mult_ref, coup_ref, list_ref, out_ref, slot_ref, held, gathered, panels, partial, received,
+           list_sem, held_sem, own_sem, gather_send, gather_recv, pass_send, pass_recv, part_send, part_recv):
     targets, slots, rank = held.shape[:3]
     clusters, nrhs = mult_ref.shape[:2]
     block = n_tgt * clusters
@@ -51,46 +53,54 @@
     own = pl.ds(my_tgt * clusters, clusters)
     own_copy = pltpu.make_async_copy(mult_ref, gathered.at[own], own_sem)
     own_copy.start()
+    list_copy = pltpu.make_async_copy(list_ref, slot_ref, list_sem)
+    list_copy.start()
     for k in range(min(DEPTH, targets)):
         coupling_copy(k).start()
     pl.semaphore_wait(barrier, chips + n_src - 1)
 
-    across = []
-    for hop in range(1, chips):
-        copy = pltpu.make_async_remote_copy(
-            src_ref=mult_ref, dst_ref=gathered.at[own], send_sem=gather_send.at[hop], recv_sem=gather_recv.at[hop],
-            device_id={"tgt": same_core(hop)}, device_id_type=MESH)
-        copy.start()
-        across.append(copy)
-    passed = [pltpu.make_async_remote_copy(
-        src_ref=mult_ref, dst_ref=gathered.at[own], send_sem=pass_send.at[0], recv_sem=pass_recv.at[0],
-        device_id={"tgt": sibling}, device_id_type=MESH)]
+    part = clusters // PARTS
+
+    def panel_copy(origin, piece, dest, send_sem, recv_sem, src_ref=None):
+        at = pl.ds(origin * clusters + piece * part, part)
+        return pltpu.make_async_remote_copy(
+            src_ref=gathered.at[at] if src_ref is None else src_ref, dst_ref=gathered.at[at], send_sem=send_sem,
+            recv_sem=recv_sem, device_id={"tgt": dest}, device_id_type=MESH)
+
+    across, passed = [], []
+    for piece in range(PARTS):
+        for hop in range(1, chips):
+            across.append(panel_copy(
+                my_tgt, piece, same_core(hop), gather_send.at[hop, piece], gather_recv.at[hop, piece],
+                mult_ref.at[pl.ds(piece * part, part)]))
+            across[-1].start()
+    passed.append(pltpu.make_async_remote_copy(
+        src_ref=mult_ref, dst_ref=gathered.at[own], send_sem=pass_send.at[0, 0], recv_sem=pass_recv.at[0, 0],
+        device_id={"tgt": sibling}, device_id_type=MESH))
     passed[0].start()
 
-    def fill(tgt):
-        high, low = split(gathered[pl.ds(tgt * clusters, clusters)])
-        at = pl.ds(tgt * clusters + 1, clusters)
-        panels[at, :nrhs] = high
-        panels[at, nrhs:] = low
+    def fill(tgt, piece=0, count=clusters):
+        at = tgt * clusters + piece * count
+        high, low = split(gathered[pl.ds(at, count)])
+        panels[pl.ds(at + 1, count), :nrhs] = high
+        panels[pl.ds(at + 1, count), nrhs:] = low
 
     panels[0] = jnp.zeros((2 * nrhs, rank), jnp.bfloat16)
+    list_copy.wait()
     own_copy.wait()
     fill(my_tgt)
     passed[0].wait_recv()
     fill(sibling)
-    for hop in range(1, chips):
-        across[hop - 1].wait_recv()
+    pieces = [(piece, hop) for piece in range(PARTS) for hop in range(1, chips)]
+    for number, (piece, hop) in enumerate(pieces):
+        across[number].wait_recv()
         origin = lax.rem(my_chip + chips - hop, chips) * 2 + my_core
-        at = gathered.at[pl.ds(origin * clusters, clusters)]
-        copy = pltpu.make_async_remote_copy(
-            src_ref=at, dst_ref=at, send_sem=pass_send.at[hop], recv_sem=pass_recv.at[hop],
-            device_id={"tgt": sibling}, device_id_type=MESH)
-        copy.start()
-        passed.append(copy)
-        fill(origin)
-    for hop in range(1, chips):
-        passed[hop].wait_recv()
-        fill(lax.rem(my_chip + chips - hop, chips) * 2 + 1 - my_core)
+        passed.append(panel_copy(origin, piece, sibling, pass_send.at[hop, piece], pass_recv.at[hop, piece]))
+        passed[-1].start()
+        fill(origin, piece, part)
+    for number, (piece, hop) in enumerate(pieces):
+        passed[number + 1].wait_recv()
+        fill(lax.rem(my_chip + chips - hop, chips) * 2 + 1 - my_core, piece, part)
 
     before = my_src * block - 1
 
@@ -100,37 +110,41 @@
             send_sem=part_send.at[dest], recv_sem=part_recv.at[my_src],
             device_id={"src": dest}, device_id_type=MESH)
 
-    def one_target(k, carry):
-        @pl.when(k + DEPTH < targets)
-        def _():
-            coupling_copy(k + DEPTH).start()
-
-        target = target_at(k)
-        coupling_copy(k).wait()
+    def one_target(target, couplings):
         total = jnp.zeros((2 * nrhs, 2 * rank), jnp.float32)
-        for first in range(0, slots, 2):
-            pair = range(first, min(first + 2, slots))
-            chosen = []
-            for s in pair:
-                chosen.append(panels[jnp.maximum(slot_ref[target, s] - before, 0)])
-            left = jnp.concatenate(chosen, axis=1)
-            high, low = split(held[k, first:first + len(pair)].reshape(len(pair) * rank, rank))
-            right = jnp.concatenate([high, low], axis=1)
+        for s in range(slots):
+            left = panels[jnp.maximum(slot_ref[target, s] - before, 0)]
+            right = jnp.concatenate(split(couplings[s]), axis=1)
             total = total + jnp.dot(left, right, preferred_element_type=jnp.float32)
         total = total[:nrhs] + total[nrhs:]
         partial[pl.ds(pl.multiple_of(target * nrhs, 8), nrhs)] = total[:, :rank] + total[:, rank:]
 
-        step = k // per_step
-        group = lax.rem(my_group + 1 + step, steps)
-
-        @pl.when(jnp.logical_and(lax.rem(k, per_step) == per_step - 1, step < steps - 1))
-        def _():
-            for o in range(owners):
-                part_copy(group * owners + o).start()
+    def one_turn(turn, carry):
+        for k in range(UNROLL):
+            k = turn * UNROLL + k
+
+            @pl.when(k + DEPTH < targets)
+            def _():
+                coupling_copy(k + DEPTH).start()
+
+        for k in range(UNROLL):
+            coupling_copy(turn * UNROLL + k).wait()
+        for k in range(UNROLL):
+            k = turn * UNROLL + k
+            one_target(target_at(k), held.at[k])
+        for k in range(UNROLL):
+            k = turn * UNROLL + k
+            step = k // per_step
+            group = lax.rem(my_group + 1 + step, steps)
+
+            @pl.when(jnp.logical_and(lax.rem(k, per_step) == per_step - 1, step < steps - 1))
+            def _():
+                for o in range(owners):
+                    part_copy(group * owners + o).start()
 
         return carry
 
-    lax.fori_loop(0, targets, one_target, 0)
+    lax.fori_loop(0, targets // UNROLL, one_turn, 0)
     for o in range(1, owners):
         part_copy(my_group * owners + lax.rem(my_place + o, owners)).start()
 
@@ -159,23 +173,25 @@
         functools.partial(kernel, n_tgt, n_src),
         out_shape=jax.ShapeDtypeStruct((rows, rank), jnp.float32),
         in_specs=[
-            pl.BlockSpec(memory_space=pl.ANY),
-            pl.BlockSpec(memory_space=pl.ANY),
-            pl.BlockSpec(memory_space=pltpu.SMEM),
+            pl.BlockSpec(memory_space=pltpu.HBM),
+            pl.BlockSpec(memory_space=pltpu.HBM),
+            pl.BlockSpec(memory_space=pltpu.HBM),
         ],
         out_specs=pl.BlockSpec(memory_space=pltpu.VMEM),
         scratch_shapes=[
+            pltpu.SMEM((targets, slots), jnp.int32),
             pltpu.VMEM((targets, slots, rank, rank), jnp.float32),
             pltpu.VMEM((n_tgt * clusters, nrhs, rank), jnp.float32),
             pltpu.VMEM((n_tgt * clusters + 1, 2 * nrhs, rank), jnp.bfloat16),
             pltpu.VMEM((targets * nrhs, rank), jnp.float32),
             pltpu.VMEM((n_src, rows, rank), jnp.float32),
+            dma,
             dma((targets,)),
             dma,
-            dma((chips,)),
-            dma((chips,)),
-            dma((chips,)),
-            dma((chips,)),
+            dma((chips, PARTS)),
+            dma((chips, PARTS)),
+            dma((chips, PARTS)),
+            dma((chips, PARTS)),
             dma((n_src,)),
             dma((n_src,)),
         ],

time: 25.1 us -> 21.9 us (0.87)
  Pallas kernels: 22.7 us -> 19.5 us
    pallas_call x1, Pallas kernels: 22.7 us -> 19.5 us  [body(): pl.pallas_call(functools.partial(kernel, n_tgt, n_src), out_shape=jax.Sha...]
where the time goes in v2:
time: 21.9 us; the launch traced here: 21.7 us
  Pallas kernels  19.5 us (89%)
  local copies, waits for them, and re-layouts  2.21 us (10%)
    pallas_call x1, Pallas kernels, body(): pl.pallas_call(functools.partial(kernel, n_tgt, n_src), out_shape=jax.Sha...  19.5 us
    unnamed x5, local copies, waits for them, and re-layouts  2.21 us

profile of v2, /device:TPU:0, one launch (start us, length us, event | category | flops | bytes accessed | tf_op | source)
XLA Modules:
  0.0 21.7 jit_solution(10176543119680558165)
XLA Ops:
  0.0 0.0 copy-start
  0.0 0.9 %copy-done = f32[16,16,128]{2,1,0:T(8,128)S(1)} copy-done((f32[16,16,128]{2,1,0:T(8,128)S(1)}, f32[16,16,128]{2,1,0:T(8,128)}, u32[]{:S(2)}) %copy-start) | copy-done | bytes 131096
  0.9 0.0 copy-start.1
  0.9 0.7 %copy-done.1 = s32[16,36]{1,0:T(8,128)S(1)} copy-done((s32[16,36]{1,0:T(8,128)S(1)}, s32[16,36]{1,0:T(8,128)}, u32[]{:S(2)}) %copy-start.1) | copy-done | bytes 2328
  1.6 19.5 %shard_map.37 = f32[32,128]{1,0:T(8,128)S(1)} custom-call(f32[16,16,128]{2,1,0:T(8,128)S(1)} %copy-done, f32[16,36,128,128]{3,2,1,0:T(8,128)} %coup_ref.1, s32[16,36]{1,0:T(8,128)S(1)} %copy-done.1), custom_call_target="tpu_custom_call" | custom-call | flops 301989888 | bytes 37748736 | tf_op jit(solution)/shard_map/pallas_call | solution.py:172
  21.1 0.6 %copy.5 = f32[32,128]{1,0:T(8,128)} copy(f32[32,128]{1,0:T(8,128)S(1)} %shard_map.37) | data formatting | bytes 32768
Async XLA Ops:
  0.0 0.9 %copy-start = (f32[16,16,128]{2,1,0:T(8,128)S(1)}, f32[16,16,128]{2,1,0:T(8,128)}, u32[]{:S(2)}) copy-start(f32[16,16,128]{2,1,0:T(8,128)} %mult_ref.1) | copy-start | bytes 393220
  0.9 0.7 %copy-start.1 = (s32[16,36]{1,0:T(8,128)S(1)}, s32[16,36]{1,0:T(8,128)}, u32[]{:S(2)}) copy-start(s32[16,36]{1,0:T(8,128)} %list_ref.1) | copy-start | bytes 6916

commit v3 on v2

--- a/solution.py
+++ b/solution.py
@@ -8,8 +8,8 @@
 from jax.sharding import PartitionSpec as P
 
 MESH = pl.DeviceIdType.MESH
-DEPTH = 8
-UNROLL = 2
+DEPTH = 12
+UNROLL = 4
 PARTS = 1
 
 

time: 21.9 us -> 21.4 us (0.977)
  Pallas kernels: 19.5 us -> 19 us
    pallas_call x1, Pallas kernels: 19.5 us -> 19 us  [body(): pl.pallas_call(functools.partial(kernel, n_tgt, n_src), out_shape=jax.Sha...]
where the time goes in v3:
time: 21.4 us; the launch traced here: 21.2 us
  Pallas kernels  19 us (89%)
  local copies, waits for them, and re-layouts  2.21 us (10%)
    pallas_call x1, Pallas kernels, body(): pl.pallas_call(functools.partial(kernel, n_tgt, n_src), out_shape=jax.Sha...  19 us
    unnamed x5, local copies, waits for them, and re-layouts  2.21 us

profile of v3, /device:TPU:0, one launch (start us, length us, event | category | flops | bytes accessed | tf_op | source)
XLA Modules:
  0.0 21.2 jit_solution(5616277554115252307)
XLA Ops:
  0.0 0.0 copy-start
  0.0 0.9 %copy-done = f32[16,16,128]{2,1,0:T(8,128)S(1)} copy-done((f32[16,16,128]{2,1,0:T(8,128)S(1)}, f32[16,16,128]{2,1,0:T(8,128)}, u32[]{:S(2)}) %copy-start) | copy-done | bytes 131096
  0.9 0.0 copy-start.1
  0.9 0.7 %copy-done.1 = s32[16,36]{1,0:T(8,128)S(1)} copy-done((s32[16,36]{1,0:T(8,128)S(1)}, s32[16,36]{1,0:T(8,128)}, u32[]{:S(2)}) %copy-start.1) | copy-done | bytes 2328
  1.6 19.0 %shard_map.37 = f32[32,128]{1,0:T(8,128)S(1)} custom-call(f32[16,16,128]{2,1,0:T(8,128)S(1)} %copy-done, f32[16,36,128,128]{3,2,1,0:T(8,128)} %coup_ref.1, s32[16,36]{1,0:T(8,128)S(1)} %copy-done.1), custom_call_target="tpu_custom_call" | custom-call | flops 301989888 | bytes 37748736 | tf_op jit(solution)/shard_map/pallas_call | solution.py:172
  20.6 0.6 %copy.5 = f32[32,128]{1,0:T(8,128)} copy(f32[32,128]{1,0:T(8,128)S(1)} %shard_map.37) | data formatting | bytes 32768
Async XLA Ops:
  0.0 0.9 %copy-start = (f32[16,16,128]{2,1,0:T(8,128)S(1)}, f32[16,16,128]{2,1,0:T(8,128)}, u32[]{:S(2)}) copy-start(f32[16,16,128]{2,1,0:T(8,128)} %mult_ref.1) | copy-start | bytes 393220
  0.9 0.7 %copy-start.1 = (s32[16,36]{1,0:T(8,128)S(1)}, s32[16,36]{1,0:T(8,128)}, u32[]{:S(2)}) copy-start(s32[16,36]{1,0:T(8,128)} %list_ref.1) | copy-start | bytes 6916
